TPU v7x, 32 devices: a whole 2x2x4 slice. The times are simulated.
32 devices in a mesh: grp: 4 (over y, x), dev: 8 (over z, core).
Axes of the slice: x: 2, y: 2, z: 4, core: 2. Of those that a mesh axis runs over, the one named last changes fastest.
Arguments:
- positions: float32 [3, 8192], P(None, ('grp', 'dev')), may hold values from -1 to 1
- velocities: float32 [3, 8192], P(None, ('grp', 'dev')), may hold values from -4 to 4
- accel_old: float32 [3, 8192], P(None, ('grp', 'dev')), may hold values from -6 to 6
- jerk_old: float32 [3, 8192], P(None, ('grp', 'dev')), may hold values from -6 to 6
- masses: float32 [8192], P(('grp', 'dev')), may hold values from 2.4414063e-05 to 0.00061035156
- levels: int32 [8192], P(('grp', 'dev')), may hold values from 0 to 3
- live_count: int32 [32], P(('grp', 'dev')), may hold values from 128 to 256, as said below
- active_slot: int32 [4096], P(('grp', 'dev')), may hold values from 0 to 255, as said below
Outputs:
- pos_vel: float32 [6, 4096], P(None, ('grp', 'dev'))
- acc_jerk: float32 [6, 4096], P(None, ('grp', 'dev'))
- potential: float32 [4096], P(('grp', 'dev'))
Inputs may be any that keep to these rules, and one draw needn't show every extreme that they name: `live_count`: every entry is at least 128; some device is full with 256 and some has exactly 128; the counts are uneven across devices. `active_slot`: within each device's aligned block of 128 entries the slots are distinct and below that device's live_count.
All inputs are finite; a program needn't handle non-finite values.
Results may differ from a plain program's by a relative error of at most 0.00029.
Values sent between devices are 32-bit elements; how exact they have to be, the bound alone decides.
A program may use at most 64 MiB of HBM per device.

v0:
```python
import jax
import jax.numpy as jnp
from jax import lax
from jax.sharding import PartitionSpec as P

tau_base = 0.5
soften_sq = 0.0001


def pair_terms(active_state, src_pos, src_vel, src_mass):
    delta_pos = src_pos[:, None, :] - active_state[0:3, :, None]
    delta_vel = src_vel[:, None, :] - active_state[3:6, :, None]
    dist_sq = jnp.sum(delta_pos * delta_pos, axis=0) + soften_sq
    weight = src_mass[None, :] / jnp.sqrt(dist_sq)
    cubed = weight / dist_sq
    radial = 3.0 * jnp.sum(delta_pos * delta_vel, axis=0) / dist_sq
    accel = jnp.sum(cubed[None] * delta_pos, axis=2)
    jerk_new = jnp.sum(cubed[None] * (delta_vel - radial[None] * delta_pos), axis=2)
    pot_sum = -jnp.sum(weight, axis=1)
    return jnp.concatenate([accel, jerk_new, pot_sum[None]], axis=0)


def correct(state, summed):
    pos_now = state[0:3]
    vel_now = state[3:6]
    acc_start = state[6:9]
    jerk_start = state[9:12]
    step_size = state[12:13]
    acc_end = summed[0:3]
    jerk_end = summed[3:6]
    differ = acc_start - acc_end
    fourth = -6.0 * differ - step_size * (4.0 * jerk_start + 2.0 * jerk_end)
    fifth = 12.0 * differ + 6.0 * step_size * (jerk_start + jerk_end)
    new_pos = (
        pos_now + step_size * step_size / 24.0 * fourth + step_size * step_size / 120.0 * fifth
    )
    new_vel = vel_now + step_size / 6.0 * fourth + step_size / 24.0 * fifth
    return (jnp.concatenate([new_pos, new_vel], axis=0), summed[0:6], summed[6])


def sweep_sources(active_state, pos_pred, vel_pred, live_mass):
    n_active = active_state.shape[1]
    block_size = min(512, n_active)
    blocks = active_state.reshape(6, n_active // block_size, block_size).transpose(1, 0, 2)

    def one_block(block):
        return pair_terms(block, pos_pred, vel_pred, live_mass)

    partial_value = lax.map(one_block, blocks)
    return partial_value.transpose(1, 0, 2).reshape(7, n_active)


def shards(positions, velocities, accel_old, jerk_old, masses, levels, live_count, active_slot):
    elapsed = tau_base * jnp.exp2(-levels.astype(jnp.float32))
    pos_pred = positions + elapsed * (
        velocities + elapsed * (accel_old / 2.0 + elapsed * jerk_old / 6.0)
    )
    vel_pred = velocities + elapsed * (accel_old + elapsed * jerk_old / 2.0)
    slots = jnp.arange(positions.shape[1], dtype=jnp.int32)
    live_mass = jnp.where(slots < live_count[0], masses, jnp.float32(0.0))
    owned = jnp.concatenate(
        [
            pos_pred[:, active_slot],
            vel_pred[:, active_slot],
            accel_old[:, active_slot],
            jerk_old[:, active_slot],
            elapsed[active_slot][None],
        ],
        axis=0,
    )
    active = lax.all_gather(owned[0:6], ("grp", "dev"), axis=1, tiled=True)
    partial_value = sweep_sources(active, pos_pred, vel_pred, live_mass)
    n_grp = lax.axis_size("grp")
    n_dev = lax.axis_size("dev")
    own_count = owned.shape[1]
    reordered = (
        partial_value.reshape(7, n_grp, n_dev, own_count)
        .transpose(0, 2, 1, 3)
        .reshape(7, n_grp * n_dev * own_count)
    )
    dev_part = lax.psum_scatter(reordered, "dev", scatter_dimension=1, tiled=True)
    summed = lax.psum_scatter(dev_part, "grp", scatter_dimension=1, tiled=True)
    return correct(owned, summed)


def solution(mesh):
    return jax.shard_map(
        shards,
        mesh=mesh,
        in_specs=(
            P(None, ("grp", "dev")),
            P(None, ("grp", "dev")),
            P(None, ("grp", "dev")),
            P(None, ("grp", "dev")),
            P(("grp", "dev")),
            P(("grp", "dev")),
            P(("grp", "dev")),
            P(("grp", "dev")),
        ),
        out_specs=(P(None, ("grp", "dev")), P(None, ("grp", "dev")), P(("grp", "dev"))),
        check_vma=False,
    )
```

profile of v0, /device:TPU:0, one launch (start us, length us, event | category | flops | bytes accessed | tf_op | source)
XLA Modules:
  0.0 130.1 jit_solution(11760795034854166556)
XLA Ops:
  7.2 0.0 copy-start.2
  7.2 0.0 reduce-scatter.3.cloned.1.call-start
  7.2 0.7 compare_select_fusion
  7.9 0.7 exponential_multiply_fusion
  8.6 0.8 multiply_add_fusion
  9.3 0.1 copy.103
  9.5 0.7 gather_fusion
  10.1 0.1 copy.104
  10.2 0.2 copy.107
  10.3 0.7 gather_fusion.3
  11.0 0.1 copy.108
  11.1 43.8 %all_gather.3 = f32[6,4096]{1,0:T(8,128)S(1)} all-gather(f32[6,128]{1,0:T(8,128)S(1)} %pad_maximum_fusion), channel_id=1, replica_groups=mesh['grp'=4,'dev'=8] {'grp','dev'}, dimensions={1}, use_global_device_ids=true | all-gather | bytes 101376 | tf_op jit(solution)/shard_map/all_gather | solution.py:71
  55.5 0.0 copy-done.2
  55.5 13.6 %while.10 = (s32[]{:T(128)}, f32[8,7,512]{2,1,0:T(8,128)S(1)}, f32[256]{0:T(256)S(1)}, f32[3,256]{1,0:T(4,128)S(1)}, f32[8,6,512]{2,1,0:T(8,128)S(1)}, /*index=5*/f32[3,256]{1,0:T(4,128)S(1)}, s32[]{:T(128)}, s32[]{:T(128)}, s32[]{}) while((s32[]{:T(128)}, f32[8,7,512]{2,1,0:T(8,128)S(1)}, f32[256]{0:T(256)S(1)}, f32[3,256]{1,0:T(4,128)S(1)}, ...), condition=%wide.region_6.7_spmd, body=%wide.region_0.6_spmd.sunk | while | flops 6033411 | bytes 4310133 | solution.py:49
  55.5 0.5 fusion.19
  56.0 0.2 fusion.20
  56.3 0.9 fusion.21
  57.2 0.5 fusion.19
  57.7 0.2 fusion.20
  58.0 0.9 fusion.21
  59.0 0.5 fusion.19
  59.4 0.2 fusion.20
  59.7 0.9 fusion.21
  60.7 0.5 fusion.19
  61.1 0.2 fusion.20
  61.4 0.9 fusion.21
  62.4 0.5 fusion.19
  62.8 0.2 fusion.20
  63.1 0.9 fusion.21
  64.1 0.5 fusion.19
  64.5 0.2 fusion.20
  64.8 0.9 fusion.21
  65.8 0.5 fusion.19
  66.2 0.2 fusion.20
  66.5 0.9 fusion.21
  67.5 0.5 fusion.19
  67.9 0.2 fusion.20
  68.2 0.9 fusion.21
  69.1 0.1 copy.110
  69.2 0.0 copy-start
  69.3 0.0 copy-start.1
  69.3 0.7 reshape.80
  70.0 0.0 reduce-scatter.3.cloned.1.call-update
  70.0 0.0 reduce-scatter.5.cloned.1.call-start
  70.1 1.3 gather_fusion.1
  71.3 25.3 %reduce-scatter.3.cloned.1.call-done = f32[7,512]{1,0:T(8,128)} async-done(((f32[7,4096]{1,0:T(8,128)}), f32[7,512]{1,0:T(8,128)}) %reduce-scatter.3.cloned.1.call-update) | async-done | bytes 14352 | tf_op jit(solution)/shard_map/reduce_scatter | solution.py:81
  96.6 0.0 reduce-scatter.5.cloned.1.call-update
  96.7 0.0 copy-done
  96.7 0.1 copy.105
  96.8 0.0 copy-done.1
  96.8 0.1 copy.112
  97.0 0.7 gather_fusion.2
  97.6 0.1 copy.106
  97.7 0.7 gather_fusion.4
  98.4 0.1 copy.113
  98.4 22.3 %reduce-scatter.5.cloned.1.call-done = f32[7,128]{1,0:T(8,128)} async-done(((f32[7,512]{1,0:T(8,128)}), f32[7,128]{1,0:T(8,128)}) %reduce-scatter.5.cloned.1.call-update) | async-done | bytes 3600 | tf_op jit(solution)/shard_map/reduce_scatter | solution.py:82
  120.7 0.8 multiply_add_fusion.3
  121.5 0.6 pad_maximum_fusion.1
  122.1 1.2 slice_bitcast_fusion
  (32 shorter events, 0.3 us)
Async XLA Ops:
  7.2 48.3 %copy-start.2 = (f32[256]{0:T(256)S(1)}, f32[256]{0:T(256)}, u32[]{:S(2)}) copy-start(f32[256]{0:T(256)} %param.14) | copy-start | bytes 3076
  7.2 89.5 %reduce-scatter.3.cloned.1.call-start = ((), (), s32[]{:S(2)}) async-start(), calls=%async_computation.2 | async-start | bytes 147456 | tf_op jit(solution)/shard_map/reduce_scatter | solution.py:81
  69.2 27.4 %copy-start = (f32[3,256]{1,0:T(4,128)S(1)}, f32[3,256]{1,0:T(4,128)}, u32[]{:S(2)}) copy-start(f32[3,256]{1,0:T(4,128)} %param.12) | copy-start | bytes 9220
  69.3 27.5 %copy-start.1 = (f32[3,256]{1,0:T(4,128)S(1)}, f32[3,256]{1,0:T(4,128)}, u32[]{:S(2)}) copy-start(f32[3,256]{1,0:T(4,128)} %param.13) | copy-start | bytes 9220
  70.0 50.7 %reduce-scatter.5.cloned.1.call-start = ((), (), s32[]{:S(2)}) async-start(), calls=%async_computation.3 | async-start | bytes 20480 | tf_op jit(solution)/shard_map/reduce_scatter | solution.py:82
Sparse Core Ops, SparseCore 0:
  70.1 26.4 reduce-scatter.2
  100.1 20.4 reduce-scatter.4
where the time goes:
time: 130 us
  waiting for transfers between devices  47.6 us (37%)
  blocking collectives  43.8 us (34%)
  other arithmetic  16.7 us (13%)
  between operations  14.8 us (11%)
  local copies, waits for them, and re-layouts  6.8 us (5%)
    all_gather x1, blocking collectives, shards(): active = lax.all_gather(owned[0:6], ('grp', 'dev'), axis=1, tiled=True)  43.8 us
    reduce_scatter x1, waiting for transfers between devices, shards(): lax.psum_scatter(reordered, 'dev', scatter_dimension=1, tiled=True)  25.3 us
    reduce_scatter x1, waiting for transfers between devices, shards(): summed = lax.psum_scatter(dev_part, 'grp', scatter_dimension=1, tiled=True)  22.3 us
    reduce_sum x8, other arithmetic, pair_terms(): accel = jnp.sum(cubed[None] * delta_pos, axis=2)  7.42 us
    reduce_sum x8, other arithmetic, pair_terms(): radial = 3.0 * jnp.sum(delta_pos * delta_vel, axis=0) / dist_sq  3.8 us
  transfers between devices with their start and end apart: 2, of which 2 were waited for; matrix products, arithmetic and copies ran while one was open for 2% of the time, Pallas kernels for 0%

commit v1 on v0

v1 whole, which is shorter than its diff:
```python
import functools
import math

import jax
import jax.numpy as jnp
from jax import lax
from jax.experimental import pallas as pl
from jax.experimental.pallas import tpu as pltpu
from jax.sharding import PartitionSpec as P

MESH = pl.DeviceIdType.MESH
LANES = 128
TAU_BASE = 0.5
SOFTEN_SQ = 0.0001


def kernel(
    n_grp, n_dev, rows, batch,
    pos_ref, vel_ref, acc_ref, jerk_ref, mass_ref, level_ref, live_ref, slot_ref,
    pos_vel_ref, acc_jerk_ref, pot_ref,
    src, rest, act, total, send_sem, recv_sem,
):
    n = n_grp * n_dev
    n_src = pos_ref.shape[1]
    n_act = slot_ref.shape[1]
    me = lax.axis_index("grp") * n_dev + lax.axis_index("dev")

    def place(index):
        return (index // n_dev, lax.rem(index, n_dev))

    barrier = pltpu.get_barrier_semaphore()

    def greet(k, carry):
        pl.semaphore_signal(
            barrier, inc=1, device_id=place(lax.rem(me + k, n)), device_id_type=MESH
        )
        return carry

    lax.fori_loop(1, n, greet, 0)

    level = level_ref[...]
    step = jnp.full(level.shape, TAU_BASE, jnp.float32)
    step = jnp.where((level & 1) != 0, step * 0.5, step)
    step = jnp.where((level & 2) != 0, step * 0.25, step)
    step = jnp.where((level & 4) != 0, step * 0.0625, step)
    vel, acc, jerk = vel_ref[...], acc_ref[...], jerk_ref[...]
    pos_pred = pos_ref[...] + step * (vel + step * (acc * 0.5 + step * jerk * (1.0 / 6.0)))
    vel_pred = vel + step * (acc + step * jerk * 0.5)
    lane = lax.broadcasted_iota(jnp.int32, (1, n_src), 1)
    live_mass = jnp.where(lane < live_ref[0], mass_ref[...], 0.0)
    src[me, 0:3, :] = pos_pred
    src[me, 3:6, :] = vel_pred
    src[me, 6:7, :] = live_mass
    src[me, 7:8, :] = jnp.zeros_like(live_mass)
    rest[0:3, :] = acc
    rest[3:6, :] = jerk
    rest[6:7, :] = step
    rest[7:8, :] = jnp.zeros_like(step)

    pl.semaphore_wait(barrier, n - 1)

    def copy(index, other):
        return pltpu.make_async_remote_copy(
            src_ref=src.at[index],
            dst_ref=src.at[index],
            send_sem=send_sem.at[other],
            recv_sem=recv_sem.at[index],
            device_id=place(other),
            device_id_type=MESH,
        )

    def send(k, carry):
        copy(me, lax.rem(me + k, n)).start()
        return carry

    lax.fori_loop(1, n, send, 0)

    slot = jnp.broadcast_to(slot_ref[...], (8, n_act))
    low, part = slot & (LANES - 1), slot // LANES

    def pick(table):
        out = jnp.zeros((8, n_act), jnp.float32)
        for chunk in range(n_src // LANES):
            found = jnp.take_along_axis(table[:, chunk * LANES : (chunk + 1) * LANES], low, axis=1)
            out = jnp.where(part == chunk, found, out)
        return out

    state = pick(src[me])
    old = pick(rest[...])
    for c in range(6):
        act[c] = jnp.broadcast_to(state[c : c + 1], (LANES, n_act)).T
    total[...] = jnp.zeros_like(total)

    def sweep(turn, carry):
        blocks = []
        for b in range(batch):
            k = turn * batch + b
            index = lax.rem(me - k + n, n)
            blocks.append(index)

            @pl.when(k > 0)
            def _():
                copy(index, index).wait_recv()

        def group(g, carry):
            at = pl.ds(pl.multiple_of(g * rows, rows), rows)
            x, y, z, vx, vy, vz = [act[c, at, :] for c in range(6)]
            ax, ay, az, jx, jy, jz, pot = [total[c, at, :] for c in range(7)]
            for index in blocks:
                for chunk in range(n_src // LANES):
                    sx, sy, sz, svx, svy, svz, mass = [
                        src[index, c : c + 1, chunk * LANES : (chunk + 1) * LANES] for c in range(7)
                    ]
                    dx, dy, dz = sx - x, sy - y, sz - z
                    ex, ey, ez = svx - vx, svy - vy, svz - vz
                    inv = lax.rsqrt(dx * dx + dy * dy + dz * dz + SOFTEN_SQ)
                    inv_sq = inv * inv
                    w = mass * inv
                    u = w * inv_sq
                    radial = (3.0 * inv_sq) * (dx * ex + dy * ey + dz * ez)
                    px, py, pz = u * dx, u * dy, u * dz
                    ax, ay, az = ax + px, ay + py, az + pz
                    jx = jx + (u * ex - radial * px)
                    jy = jy + (u * ey - radial * py)
                    jz = jz + (u * ez - radial * pz)
                    pot = pot + w
            for c, value in enumerate((ax, ay, az, jx, jy, jz, pot)):
                total[c, at, :] = value
            return carry

        lax.fori_loop(0, n_act // rows, group, 0)
        return carry

    lax.fori_loop(0, n // batch, sweep, 0)

    for c in range(6):
        acc_jerk_ref[c : c + 1, :] = jnp.sum(total[c].T, axis=0, keepdims=True)
    pot_ref[...] = -jnp.sum(total[6].T, axis=0, keepdims=True)

    acc_end, jerk_end = acc_jerk_ref[0:3, :], acc_jerk_ref[3:6, :]
    acc_start, jerk_start, h = old[0:3], old[3:6], old[6:7]
    differ = acc_start - acc_end
    fourth = -6.0 * differ - h * (4.0 * jerk_start + 2.0 * jerk_end)
    fifth = 12.0 * differ + 6.0 * h * (jerk_start + jerk_end)
    pos_vel_ref[0:3, :] = state[0:3] + h * h * (1.0 / 24.0) * fourth + h * h * (1.0 / 120.0) * fifth
    pos_vel_ref[3:6, :] = state[3:6] + h * (1.0 / 6.0) * fourth + h * (1.0 / 24.0) * fifth

    def settle(k, carry):
        copy(me, lax.rem(me + k, n)).wait_send()
        return carry

    lax.fori_loop(1, n, settle, 0)


def solution(mesh):
    n_grp, n_dev = mesh.shape["grp"], mesh.shape["dev"]
    n = n_grp * n_dev

    def shards(positions, velocities, accel_old, jerk_old, masses, levels, live_count, active_slot):
        n_src, n_act = positions.shape[1], active_slot.shape[0]
        rows = math.gcd(16, n_act)
        batch = math.gcd(4, n)
        vmem = pl.BlockSpec(memory_space=pltpu.VMEM)
        pos_vel, acc_jerk, pot = pl.pallas_call(
            functools.partial(kernel, n_grp, n_dev, rows, batch),
            out_shape=(
                jax.ShapeDtypeStruct((6, n_act), jnp.float32),
                jax.ShapeDtypeStruct((6, n_act), jnp.float32),
                jax.ShapeDtypeStruct((1, n_act), jnp.float32),
            ),
            in_specs=[vmem] * 6 + [pl.BlockSpec(memory_space=pltpu.SMEM), vmem],
            out_specs=(vmem, vmem, vmem),
            scratch_shapes=[
                pltpu.VMEM((n, 8, n_src), jnp.float32),
                pltpu.VMEM((8, n_src), jnp.float32),
                pltpu.VMEM((6, n_act, LANES), jnp.float32),
                pltpu.VMEM((7, n_act, LANES), jnp.float32),
                pltpu.SemaphoreType.DMA((n,)),
                pltpu.SemaphoreType.DMA((n,)),
            ],
            compiler_params=pltpu.CompilerParams(
                collective_id=0, has_side_effects=True, vmem_limit_bytes=32 * 1024 * 1024
            ),
        )(
            positions, velocities, accel_old, jerk_old,
            masses[None], levels[None], live_count, active_slot[None],
        )
        return pos_vel, acc_jerk, pot[0]

    split = P(None, ("grp", "dev"))
    flat = P(("grp", "dev"))
    return jax.shard_map(
        shards,
        mesh=mesh,
        in_specs=(split, split, split, split, flat, flat, flat, flat),
        out_specs=(split, split, flat),
        check_vma=False,
    )
```

time: 130 us -> 23.6 us (0.18)
  waiting for transfers between devices: 47.6 us -> 0 us
  blocking collectives: 43.8 us -> 0 us
  Pallas kernels: 0 us -> 17.5 us
  other arithmetic: 16.7 us -> 0 us
  between operations: 14.8 us -> 1.34 us
  local copies, waits for them, and re-layouts: 6.8 us -> 4.43 us
    reduce_scatter x2 -> x0, waiting for transfers between devices: 47.6 us -> none  [the longest x1 25.3 us: shards(): lax.psum_scatter(reordered, 'dev', scatter_dimension=1, tiled=True)]
    all_gather x1 -> x0, blocking collectives: 43.8 us -> none  [shards(): active = lax.all_gather(owned[0:6], ('grp', 'dev'), axis=1, tiled=True)]
    pallas_call x0 -> x1, Pallas kernels: none -> 17.5 us  [shards(): pl.pallas_call(functools.partial(kernel, n_grp, n_dev, rows, batch), out_...]
    reduce_sum x16 -> x0, other arithmetic: 11.2 us -> none  [the longest x8 7.42 us: pair_terms(): accel = jnp.sum(cubed[None] * delta_pos, axis=2)]
    unnamed x8 -> x17, local copies, waits for them, and re-layouts: 0.28 us -> 4.43 us
    gather x9 -> x0, local copies, waits for them, and re-layouts: 4.12 us -> none  [the longest x1 1.27 us: shards(): elapsed[active_slot][None]]
    div x9 -> x0, other arithmetic: 1.82 us -> none  [the longest x8 1.82 us: pair_terms(): cubed = weight / dist_sq]
    add x3 -> x0, other arithmetic: 1.53 us -> none  [the longest x1 0.77 us: correct(): pos_now + step_size * step_size / 24.0 * fourth]
  transfers between devices with their start and end apart: 2 -> 0, of which waited for: 2 -> 0; matrix products, arithmetic and copies ran while one was open for 2% -> 0% of each run, Pallas kernels for 0% -> 0%
where the time goes in v1:
time: 23.6 us; the launch traced here: 23.3 us
  Pallas kernels  17.5 us (74%)
  local copies, waits for them, and re-layouts  4.43 us (19%)
  between operations  1.34 us (6%)
    pallas_call x1, Pallas kernels, shards(): pl.pallas_call(functools.partial(kernel, n_grp, n_dev, rows, batch), out_...  17.5 us
    unnamed x17, local copies, waits for them, and re-layouts  4.43 us

profile of v1, /device:TPU:0, one launch (start us, length us, event | category | flops | bytes accessed | tf_op | source)
XLA Modules:
  0.0 23.3 jit_solution(11553307181668116085)
XLA Ops:
  0.6 0.0 copy-start
  1.3 0.0 copy-start.5
  1.3 0.0 copy-start.4
  1.3 0.0 copy-start.6
  1.3 0.0 copy-done
  1.3 0.6 %copy-done.5 = s32[256]{0:T(256)S(1)} copy-done((s32[256]{0:T(256)S(1)}, s32[256]{0:T(256)}, u32[]{:S(2)}) %copy-start.5) | copy-done | bytes 1048
  2.0 0.0 copy-done.4
  2.0 0.0 copy-done.6
  2.0 0.0 copy-start.1
  2.0 0.7 %copy-done.1 = f32[3,256]{1,0:T(4,128)S(1)} copy-done((f32[3,256]{1,0:T(4,128)S(1)}, f32[3,256]{1,0:T(4,128)}, u32[]{:S(2)}) %copy-start.1) | copy-done | bytes 3096
  2.7 0.0 copy-start.2
  2.7 0.7 %copy-done.2 = f32[3,256]{1,0:T(4,128)S(1)} copy-done((f32[3,256]{1,0:T(4,128)S(1)}, f32[3,256]{1,0:T(4,128)}, u32[]{:S(2)}) %copy-start.2) | copy-done | bytes 3096
  3.4 0.0 copy-start.3
  3.4 0.7 %copy-done.3 = f32[3,256]{1,0:T(4,128)S(1)} copy-done((f32[3,256]{1,0:T(4,128)S(1)}, f32[3,256]{1,0:T(4,128)}, u32[]{:S(2)}) %copy-start.3) | copy-done | bytes 3096
  4.1 17.5 %shard_map.103 = (f32[6,128]{1,0:T(8,128)S(1)}, f32[6,128]{1,0:T(8,128)S(1)}, f32[1,128]{1,0:T(1,128)S(1)}) custom-call(f32[3,256]{1,0:T(4,128)S(1)} %copy-done, f32[3,256]{1,0:T(4,128)S(1)} %copy-done.1, f32[3,256]{1,0:T(4,128)S(1)} %copy-done.2, f32[3,256]{1,0:T(4,128)S(1)} %copy-done.3, f32[1,256]{1,0:T(1,128)S(1)} %bitcast.4, s32[1,256]{1,0:T(1,128)S(1)} %bitcast.5, ...), custom_call_target="tpu_custom_call" | custom-call | tf_op jit(solution)/shard_map/pallas_call | solution.py:164
  21.6 0.6 %copy.15 = f32[6,128]{1,0:T(8,128)} copy(f32[6,128]{1,0:T(8,128)S(1)} %get-tuple-element.12) | data formatting | bytes 6144
  22.2 0.6 %copy.16 = f32[6,128]{1,0:T(8,128)} copy(f32[6,128]{1,0:T(8,128)S(1)} %get-tuple-element.13) | data formatting | bytes 6144
  22.8 0.5 %copy.17 = f32[128]{0:T(128)} copy(f32[128]{0:T(128)S(1)} %bitcast.7) | data formatting | bytes 1024
Async XLA Ops:
  0.6 0.7 %copy-start = (f32[3,256]{1,0:T(4,128)S(1)}, f32[3,256]{1,0:T(4,128)}, u32[]{:S(2)}) copy-start(f32[3,256]{1,0:T(4,128)} %pos_ref.1) | copy-start | bytes 9220
  1.3 0.7 %copy-start.5 = (s32[256]{0:T(256)S(1)}, s32[256]{0:T(256)}, u32[]{:S(2)}) copy-start(s32[256]{0:T(256)} %param.13) | copy-start | bytes 3076
  1.3 0.7 %copy-start.4 = (f32[256]{0:T(256)S(1)}, f32[256]{0:T(256)}, u32[]{:S(2)}) copy-start(f32[256]{0:T(256)} %param.12) | copy-start | bytes 3076
  1.3 0.7 %copy-start.6 = (s32[128]{0:T(128)S(1)}, s32[128]{0:T(128)}, u32[]{:S(2)}) copy-start(s32[128]{0:T(128)} %param.15) | copy-start | bytes 1540
  2.0 0.7 %copy-start.1 = (f32[3,256]{1,0:T(4,128)S(1)}, f32[3,256]{1,0:T(4,128)}, u32[]{:S(2)}) copy-start(f32[3,256]{1,0:T(4,128)} %vel_ref.1) | copy-start | bytes 9220
  2.7 0.7 %copy-start.2 = (f32[3,256]{1,0:T(4,128)S(1)}, f32[3,256]{1,0:T(4,128)}, u32[]{:S(2)}) copy-start(f32[3,256]{1,0:T(4,128)} %acc_ref.1) | copy-start | bytes 9220
  3.4 0.7 %copy-start.3 = (f32[3,256]{1,0:T(4,128)S(1)}, f32[3,256]{1,0:T(4,128)}, u32[]{:S(2)}) copy-start(f32[3,256]{1,0:T(4,128)} %jerk_ref.1) | copy-start | bytes 9220

commit v2 on v1

v2 whole, which is shorter than its diff:
```python
import functools
import math

import jax
import jax.numpy as jnp
from jax import lax
from jax.experimental import pallas as pl
from jax.experimental.pallas import tpu as pltpu
from jax.sharding import PartitionSpec as P

MESH = pl.DeviceIdType.MESH
LANES = 128
TAU_BASE = 0.5
SOFTEN_SQ = 0.0001


def add_pairs(state, sums, source):
    x, y, z, vx, vy, vz = state
    ax, ay, az, jx, jy, jz, pot = sums
    sx, sy, sz, svx, svy, svz, mass = source
    dx, dy, dz = sx - x, sy - y, sz - z
    ex, ey, ez = svx - vx, svy - vy, svz - vz
    inv = lax.rsqrt(dx * dx + dy * dy + dz * dz + SOFTEN_SQ)
    inv_sq = inv * inv
    w = mass * inv
    u = w * inv_sq
    radial = (3.0 * inv_sq) * (dx * ex + dy * ey + dz * ez)
    px, py, pz = u * dx, u * dy, u * dz
    return (
        ax + px, ay + py, az + pz,
        jx + (u * ex - radial * px), jy + (u * ey - radial * py), jz + (u * ez - radial * pz),
        pot + w,
    )


def sweep(act, total, rows, chunks):
    def group(g, carry):
        at = pl.ds(pl.multiple_of(g * rows, rows), rows)
        state = [act[c, at, :] for c in range(6)]
        sums = tuple(total[c, at, :] for c in range(7))
        for chunk in chunks:
            sums = add_pairs(state, sums, [chunk(c) for c in range(7)])
        for c in range(7):
            total[c, at, :] = sums[c]
        return carry

    lax.fori_loop(0, act.shape[1] // rows, group, 0)


def share(
    n_grp, n_dev, rows, batch,
    pos_hbm, vel_hbm, acc_hbm, jerk_hbm, mass_hbm, level_hbm, live_hbm, slot_hbm,
    src, act, total, own,
    pos_ref, vel_ref, acc_ref, jerk_ref, mass_ref, level_ref, live_ref, slot_ref,
    rest, load_sem, send_sem, recv_sem,
):
    n = n_grp * n_dev
    n_src = pos_ref.shape[1]
    n_act = slot_ref.shape[1]
    n_chunk = n_src // LANES
    me = lax.axis_index("grp") * n_dev + lax.axis_index("dev")

    loads = [
        pltpu.make_async_copy(there, here, load_sem.at[i])
        for i, (there, here) in enumerate((
            (pos_hbm, pos_ref), (vel_hbm, vel_ref), (acc_hbm, acc_ref), (jerk_hbm, jerk_ref),
            (mass_hbm, mass_ref), (level_hbm, level_ref), (live_hbm, live_ref), (slot_hbm, slot_ref),
        ))
    ]
    for load in loads:
        load.start()

    def place(index):
        return (index // n_dev, lax.rem(index, n_dev))

    barrier = pltpu.get_barrier_semaphore()

    def greet(k, carry):
        pl.semaphore_signal(
            barrier, inc=1, device_id=place(lax.rem(me + k, n)), device_id_type=MESH
        )
        return carry

    lax.fori_loop(1, n, greet, 0)
    total[...] = jnp.zeros_like(total)
    for load in loads:
        load.wait()

    level = level_ref[...]
    step = jnp.full(level.shape, TAU_BASE, jnp.float32)
    step = jnp.where((level & 1) != 0, step * 0.5, step)
    step = jnp.where((level & 2) != 0, step * 0.25, step)
    step = jnp.where((level & 4) != 0, step * 0.0625, step)
    vel, acc, jerk = vel_ref[...], acc_ref[...], jerk_ref[...]
    pos_pred = pos_ref[...] + step * (vel + step * (acc * 0.5 + step * jerk * (1.0 / 6.0)))
    vel_pred = vel + step * (acc + step * jerk * 0.5)
    lane = lax.broadcasted_iota(jnp.int32, (1, n_src), 1)
    live = jnp.full((1, n_src), live_ref[0], jnp.int32)
    live_mass = jnp.where(lane < live, mass_ref[...], 0.0)
    count = live.astype(jnp.float32)
    for chunk in range(n_chunk):
        cut = slice(chunk * LANES, (chunk + 1) * LANES)
        src[me, chunk, 0:3, :] = pos_pred[:, cut]
        src[me, chunk, 3:6, :] = vel_pred[:, cut]
        src[me, chunk, 6:7, :] = live_mass[:, cut]
        src[me, chunk, 7:8, :] = count[:, cut]
    rest[0:3, :] = acc
    rest[3:6, :] = jerk
    rest[6:7, :] = step
    rest[7:8, :] = jnp.zeros_like(step)

    pl.semaphore_wait(barrier, n - 1)

    def copy(index, other):
        return pltpu.make_async_remote_copy(
            src_ref=src.at[index],
            dst_ref=src.at[index],
            send_sem=send_sem.at[other],
            recv_sem=recv_sem.at[index],
            device_id=place(other),
            device_id_type=MESH,
        )

    def send(k, carry):
        copy(me, lax.rem(me + k, n)).start()
        return carry

    lax.fori_loop(1, n, send, 0)

    slot = jnp.broadcast_to(slot_ref[...], (8, n_act))
    low, part = slot & (LANES - 1), slot // LANES

    def pick(chunk_of):
        out = jnp.zeros((8, n_act), jnp.float32)
        for chunk in range(n_chunk):
            found = jnp.take_along_axis(chunk_of(chunk), low, axis=1)
            out = jnp.where(part == chunk, found, out)
        return out

    state = pick(lambda chunk: src[me, chunk])
    own[0:8, :] = state
    own[8:16, :] = pick(lambda chunk: rest[:, chunk * LANES : (chunk + 1) * LANES])
    for c in range(6):
        act[c] = jnp.broadcast_to(state[c : c + 1], (LANES, n_act)).T

    def arrive(turn, carry):
        chunks = []
        for b in range(batch):
            k = turn * batch + b
            index = lax.rem(me - k + n, n)
            chunks.append(lambda c, index=index: src[index, 0, c : c + 1, :])

            @pl.when(k > 0)
            def _():
                copy(index, index).wait_recv()

        sweep(act, total, rows, chunks)
        return carry

    lax.fori_loop(0, n // batch, arrive, 0)

    def settle(k, carry):
        copy(me, lax.rem(me + k, n)).wait_send()
        return carry

    lax.fori_loop(1, n, settle, 0)


def finish(
    rows, batch,
    src, act, total, own,
    pos_vel_hbm, acc_jerk_hbm, pot_hbm,
    packed, more, pos_vel_ref, acc_jerk_ref, pot_ref, store_sem,
):
    n, n_chunk = src.shape[0], src.shape[1]
    lane = lax.broadcasted_iota(jnp.int32, (8, LANES), 1)
    row = lax.broadcasted_iota(jnp.int32, (8, LANES), 0)
    more[...] = jnp.zeros_like(more)

    unroll = math.gcd(8, n)

    def pack(turn, carry):
        filled, now = carry
        counts = [src[turn * unroll + b, 0, 7, 0].astype(jnp.int32) for b in range(unroll)]
        for b in range(unroll):
            for chunk in range(1, n_chunk):
                many = jnp.minimum(jnp.maximum(counts[b] - chunk * LANES, 0), LANES)
                start = lax.rem(filled, LANES)
                moved = pltpu.roll(src[turn * unroll + b, chunk], start, 1)
                now = jnp.where(lane >= start, moved, now)
                packed[filled // LANES] = now
                now = jnp.where(start + many >= LANES, moved, now)
                filled = filled + many
        return filled, now

    filled, now = lax.fori_loop(
        0, n // unroll, pack, (jnp.int32(0), jnp.zeros((8, LANES), jnp.float32))
    )
    last = filled // LANES
    packed[last] = jnp.where((row == 6) & (lane >= lax.rem(filled, LANES)), 0.0, now)
    for b in range(1, batch):
        packed[last + b] = jnp.zeros((8, LANES), jnp.float32)

    def turns(turn, carry):
        sweep(act, more, rows, [
            lambda c, at=turn * batch + b: packed[at, c : c + 1, :] for b in range(batch)
        ])
        return carry

    lax.fori_loop(0, (filled + batch * LANES - 1) // (batch * LANES), turns, 0)

    for c in range(6):
        acc_jerk_ref[c : c + 1, :] = jnp.sum((total[c] + more[c]).T, axis=0, keepdims=True)
    pot_ref[...] = -jnp.sum((total[6] + more[6]).T, axis=0, keepdims=True)
    stores = [
        pltpu.make_async_copy(here, there, store_sem.at[i])
        for i, (here, there) in enumerate((
            (acc_jerk_ref, acc_jerk_hbm), (pot_ref, pot_hbm), (pos_vel_ref, pos_vel_hbm),
        ))
    ]
    stores[0].start()
    stores[1].start()

    acc_end, jerk_end = acc_jerk_ref[0:3, :], acc_jerk_ref[3:6, :]
    pos_now, vel_now = own[0:3, :], own[3:6, :]
    acc_start, jerk_start, h = own[8:11, :], own[11:14, :], own[14:15, :]
    differ = acc_start - acc_end
    fourth = -6.0 * differ - h * (4.0 * jerk_start + 2.0 * jerk_end)
    fifth = 12.0 * differ + 6.0 * h * (jerk_start + jerk_end)
    pos_vel_ref[0:3, :] = pos_now + h * h * (1.0 / 24.0) * fourth + h * h * (1.0 / 120.0) * fifth
    pos_vel_ref[3:6, :] = vel_now + h * (1.0 / 6.0) * fourth + h * (1.0 / 24.0) * fifth
    stores[2].start()
    for store in stores:
        store.wait()


def solution(mesh):
    n_grp, n_dev = mesh.shape["grp"], mesh.shape["dev"]
    n = n_grp * n_dev

    def shards(positions, velocities, accel_old, jerk_old, masses, levels, live_count, active_slot):
        n_src, n_act = positions.shape[1], active_slot.shape[0]
        n_chunk = n_src // LANES
        vmem = pl.BlockSpec(memory_space=pltpu.VMEM)
        hbm = pl.BlockSpec(memory_space=pltpu.HBM)
        args = (
            positions, velocities, accel_old, jerk_old,
            masses[None], levels[None], live_count, active_slot[None],
        )
        f32 = jnp.float32
        middle = pl.pallas_call(
            functools.partial(share, n_grp, n_dev, math.gcd(16, n_act), math.gcd(4, n)),
            out_shape=(
                jax.ShapeDtypeStruct((n, n_chunk, 8, LANES), f32),
                jax.ShapeDtypeStruct((6, n_act, LANES), f32),
                jax.ShapeDtypeStruct((7, n_act, LANES), f32),
                jax.ShapeDtypeStruct((16, n_act), f32),
            ),
            in_specs=[hbm] * 8,
            out_specs=(vmem,) * 4,
            scratch_shapes=[
                (pltpu.SMEM if a is live_count else pltpu.VMEM)(a.shape, a.dtype) for a in args
            ] + [
                pltpu.VMEM((8, n_src), f32),
                pltpu.SemaphoreType.DMA((8,)),
                pltpu.SemaphoreType.DMA((n,)),
                pltpu.SemaphoreType.DMA((n,)),
            ],
            compiler_params=pltpu.CompilerParams(
                collective_id=0, has_side_effects=True, vmem_limit_bytes=60 * 1024 * 1024
            ),
        )(*args)
        batch = 2
        pos_vel, acc_jerk, pot = pl.pallas_call(
            functools.partial(finish, math.gcd(32, n_act), batch),
            out_shape=(
                jax.ShapeDtypeStruct((6, n_act), f32),
                jax.ShapeDtypeStruct((6, n_act), f32),
                jax.ShapeDtypeStruct((1, n_act), f32),
            ),
            in_specs=[vmem] * 4,
            out_specs=(hbm,) * 3,
            scratch_shapes=[
                pltpu.VMEM((n * (n_chunk - 1) + batch, 8, LANES), f32),
                pltpu.VMEM((7, n_act, LANES), f32),
                pltpu.VMEM((6, n_act), f32),
                pltpu.VMEM((6, n_act), f32),
                pltpu.VMEM((1, n_act), f32),
                pltpu.SemaphoreType.DMA((3,)),
            ],
            compiler_params=pltpu.CompilerParams(vmem_limit_bytes=60 * 1024 * 1024),
        )(*middle)
        return pos_vel, acc_jerk, pot[0]

    split = P(None, ("grp", "dev"))
    flat = P(("grp", "dev"))
    return jax.shard_map(
        shards,
        mesh=mesh,
        in_specs=(split, split, split, split, flat, flat, flat, flat),
        out_specs=(split, split, flat),
        check_vma=False,
    )
```

time: 23.6 us -> 22.3 us (0.945)
  local copies, waits for them, and re-layouts: 4.43 us -> 0 us
  Pallas kernels: 17.5 us -> 20.9 us
    unnamed x17 -> x0, local copies, waits for them, and re-layouts: 4.43 us -> none
    pallas_call x1 -> x2, Pallas kernels: 17.5 us -> 20.9 us  [the longest x1 16.9 us: shards(): pl.pallas_call(functools.partial(share, n_grp, n_dev, math.gcd(16, n_act)...]
where the time goes in v2:
time: 22.3 us; the launch traced here: 22.2 us
  Pallas kernels  20.9 us (94%)
  between operations  1.29 us (6%)
    pallas_call x1, Pallas kernels, shards(): pl.pallas_call(functools.partial(share, n_grp, n_dev, math.gcd(16, n_act)...  16.9 us
    pallas_call x1, Pallas kernels, shards(): pl.pallas_call(functools.partial(finish, math.gcd(32, n_act), batch), out...  4 us

profile of v2, /device:TPU:0, one launch (start us, length us, event | category | flops | bytes accessed | tf_op | source)
XLA Modules:
  0.0 22.2 jit_solution(3493455277409464910)
XLA Ops:
  1.3 16.9 %shard_map.103 = (f32[32,2,8,128]{3,2,1,0:T(8,128)}, f32[6,128,128]{2,1,0:T(8,128)}, f32[7,128,128]{2,1,0:T(8,128)}, f32[16,128]{1,0:T(8,128)}) custom-call(f32[3,256]{1,0:T(4,128)} %pos_hbm.1, f32[3,256]{1,0:T(4,128)} %vel_hbm.1, f32[3,256]{1,0:T(4,128)} %acc_hbm.1, f32[3,256]{1,0:T(4,128)} %jerk_hbm.1, f32[1,256]{1,0:T(1,128)} %bitcast.4, ...), custom_call_target="tpu_custom_call" | custom-call | tf_op jit(solution)/shard_map/pallas_call | solution.py:251
  18.2 4.0 %shard_map.104 = (f32[6,128]{1,0:T(8,128)}, f32[6,128]{1,0:T(8,128)}, f32[1,128]{1,0:T(1,128)}) custom-call(f32[32,2,8,128]{3,2,1,0:T(8,128)} %get-tuple-element.10.src, f32[6,128,128]{2,1,0:T(8,128)} %get-tuple-element.11.act, f32[7,128,128]{2,1,0:T(8,128)} %get-tuple-element.12.total, f32[16,128]{1,0:T(8,128)} %get-tuple-element.13.own), custom_call_target="tpu_custom_call" | custom-call | tf_op jit(solution)/shard_map/pallas_call | solution.py:274

commit v3 on v2

v3 whole, which is shorter than its diff:
```python
import functools
import math

import jax
import jax.numpy as jnp
from jax import lax
from jax.experimental import pallas as pl
from jax.experimental.pallas import tpu as pltpu
from jax.sharding import PartitionSpec as P

MESH = pl.DeviceIdType.MESH
LANES = 128
TAU_BASE = 0.5
SOFTEN_SQ = 0.0001


def add_pairs(state, sums, source):
    x, y, z, vx, vy, vz = state
    ax, ay, az, jx, jy, jz, pot = sums
    sx, sy, sz, svx, svy, svz, mass = source
    dx, dy, dz = sx - x, sy - y, sz - z
    ex, ey, ez = svx - vx, svy - vy, svz - vz
    inv = lax.rsqrt(dx * dx + dy * dy + dz * dz + SOFTEN_SQ)
    inv_sq = inv * inv
    w = mass * inv
    u = w * inv_sq
    radial = (3.0 * inv_sq) * (dx * ex + dy * ey + dz * ez)
    px, py, pz = u * dx, u * dy, u * dz
    return (
        ax + px, ay + py, az + pz,
        jx + (u * ex - radial * px), jy + (u * ey - radial * py), jz + (u * ez - radial * pz),
        pot + w,
    )


def sweep(act, total, rows, fresh, chunks):
    def group(g, carry):
        at = pl.ds(pl.multiple_of(g * rows, rows), rows)
        state = [act[c, at, :] for c in range(6)]
        if fresh:
            sums = (jnp.zeros((rows, LANES), jnp.float32),) * 7
        else:
            sums = tuple(total[c, at, :] for c in range(7))
        for chunk in chunks:
            sums = add_pairs(state, sums, [chunk(c) for c in range(7)])
        for c in range(7):
            total[c, at, :] = sums[c]
        return carry

    lax.fori_loop(0, act.shape[1] // rows, group, 0)


def share(
    n_grp, n_dev, few, many,
    pos_hbm, vel_hbm, acc_hbm, jerk_hbm, mass_hbm, level_hbm, live_hbm, slot_hbm,
    out_hbm,
    pos_ref, vel_ref, acc_ref, jerk_ref, mass_ref, level_ref, live_ref, slot_ref,
    src, stars, act, total, rest, part, gain, out,
    load_sem, src_send, src_recv, star_send, star_recv, part_send, part_recv, out_sem,
):
    n_src = pos_ref.shape[1]
    n_act = slot_ref.shape[1]
    n_chunk = n_src // LANES
    grp, dev = lax.axis_index("grp"), lax.axis_index("dev")

    loads = [
        pltpu.make_async_copy(there, here, load_sem.at[i])
        for i, (there, here) in enumerate((
            (pos_hbm, pos_ref), (vel_hbm, vel_ref), (acc_hbm, acc_ref), (jerk_hbm, jerk_ref),
            (mass_hbm, mass_ref), (level_hbm, level_ref), (live_hbm, live_ref), (slot_hbm, slot_ref),
        ))
    ]
    for load in loads:
        load.start()

    def on_dev(k):
        return lax.rem(dev + k, n_dev)

    def on_grp(k):
        return lax.rem(grp + k, n_grp)

    def each(count, body):
        def one(k, carry):
            body(k)
            return carry

        lax.fori_loop(1, count, one, 0)

    barrier = pltpu.get_barrier_semaphore()

    def greet(place):
        pl.semaphore_signal(barrier, inc=1, device_id=place, device_id_type=MESH)

    each(n_dev, lambda k: greet((grp, on_dev(k))))
    each(n_grp, lambda k: greet((on_grp(k), dev)))
    for load in loads:
        load.wait()

    mine = src.at[dev]
    level = level_ref[...]
    step = jnp.full(level.shape, TAU_BASE, jnp.float32)
    step = jnp.where((level & 1) != 0, step * 0.5, step)
    step = jnp.where((level & 2) != 0, step * 0.25, step)
    step = jnp.where((level & 4) != 0, step * 0.0625, step)
    vel, acc, jerk = vel_ref[...], acc_ref[...], jerk_ref[...]
    pos_pred = pos_ref[...] + step * (vel + step * (acc * 0.5 + step * jerk * (1.0 / 6.0)))
    vel_pred = vel + step * (acc + step * jerk * 0.5)
    lane = lax.broadcasted_iota(jnp.int32, (1, n_src), 1)
    live_mass = jnp.where(lane < live_ref[0], mass_ref[...], 0.0)
    blank = jnp.zeros_like(step)
    for chunk in range(n_chunk):
        cut = slice(chunk * LANES, (chunk + 1) * LANES)
        mine[chunk, 0:3, :] = pos_pred[:, cut]
        mine[chunk, 3:6, :] = vel_pred[:, cut]
        mine[chunk, 6:7, :] = live_mass[:, cut]
        mine[chunk, 7:8, :] = blank[:, cut]
    rest[0:3, :] = acc
    rest[3:6, :] = jerk
    rest[6:7, :] = step
    rest[7:8, :] = blank

    pl.semaphore_wait(barrier, (n_dev - 1) + (n_grp - 1))

    def src_copy(origin, other):
        return pltpu.make_async_remote_copy(
            src_ref=src.at[origin], dst_ref=src.at[origin],
            send_sem=src_send.at[other], recv_sem=src_recv.at[origin],
            device_id=(grp, other), device_id_type=MESH,
        )

    def star_copy(origin, other):
        return pltpu.make_async_remote_copy(
            src_ref=stars.at[origin], dst_ref=stars.at[origin],
            send_sem=star_send.at[other], recv_sem=star_recv.at[origin],
            device_id=(other, dev), device_id_type=MESH,
        )

    def part_copy(origin, other):
        return pltpu.make_async_remote_copy(
            src_ref=part.at[other], dst_ref=gain.at[origin],
            send_sem=part_send.at[other], recv_sem=part_recv.at[origin],
            device_id=(other, dev), device_id_type=MESH,
        )

    each(n_dev, lambda k: src_copy(dev, on_dev(k)).start())

    slot = jnp.broadcast_to(slot_ref[...], (8, n_act))
    low, place = slot & (LANES - 1), slot // LANES

    def pick(chunk_of):
        found = jnp.zeros((8, n_act), jnp.float32)
        for chunk in range(n_chunk):
            here = jnp.take_along_axis(chunk_of(chunk), low, axis=1)
            found = jnp.where(place == chunk, here, found)
        return found

    state = pick(lambda chunk: mine[chunk])
    stars[grp] = state
    each(n_grp, lambda k: star_copy(grp, on_grp(k)).start())
    old = pick(lambda chunk: rest[:, chunk * LANES : (chunk + 1) * LANES])

    def spread(origin):
        for c in range(6):
            act[origin, c] = jnp.broadcast_to(stars[origin, c : c + 1, :], (LANES, n_act)).T

    spread(grp)

    def meet(k):
        origin = on_grp(k)
        star_copy(origin, origin).wait_recv()
        spread(origin)

    each(n_grp, meet)

    def add(origin, batch, turn, fresh, arriving):
        chunks = []
        for b in range(batch):
            k = turn * batch + b
            index = on_dev(k)
            chunks += [
                lambda c, index=index, chunk=chunk: src[index, chunk, c : c + 1, :]
                for chunk in range(n_chunk)
            ]
            if arriving and not (fresh and b == 0):
                src_copy(index, index).wait_recv()
        sweep(act.at[origin], total, math.gcd(16, n_act), fresh, chunks)

    def add_all(origin, batch, arriving):
        add(origin, batch, 0, True, arriving)

        def turns(turn, carry):
            add(origin, batch, turn, False, arriving)
            return carry

        lax.fori_loop(1, n_dev // batch, turns, 0)

    def total_of(c):
        return jnp.sum(total[c].T, axis=0, keepdims=True)

    def give(k, batch, arriving):
        origin = on_grp(k)
        add_all(origin, batch, arriving)
        for c in range(7):
            part[origin, c : c + 1, :] = total_of(c)
        part[origin, 7:8, :] = jnp.zeros((1, n_act), jnp.float32)
        part_copy(grp, origin).start()

    if n_grp > 1:
        give(1, few, True)

    def give_next(k, carry):
        give(k, many, False)
        return carry

    lax.fori_loop(2, n_grp, give_next, 0)
    add_all(grp, many, n_grp == 1)
    for c in range(7):
        part[grp, c : c + 1, :] = total_of(c)
    part[grp, 7:8, :] = jnp.zeros((1, n_act), jnp.float32)

    def gather(k, summed):
        origin = on_grp(k)
        part_copy(origin, origin).wait_recv()
        return summed + gain[origin]

    summed = lax.fori_loop(1, n_grp, gather, part[grp])

    acc_end, jerk_end = summed[0:3], summed[3:6]
    acc_start, jerk_start, h = old[0:3], old[3:6], old[6:7]
    differ = acc_start - acc_end
    fourth = -6.0 * differ - h * (4.0 * jerk_start + 2.0 * jerk_end)
    fifth = 12.0 * differ + 6.0 * h * (jerk_start + jerk_end)
    out[0, 0:3, :] = state[0:3] + h * h * (1.0 / 24.0) * fourth + h * h * (1.0 / 120.0) * fifth
    out[0, 3:6, :] = state[3:6] + h * (1.0 / 6.0) * fourth + h * (1.0 / 24.0) * fifth
    out[0, 6:8, :] = jnp.zeros((2, n_act), jnp.float32)
    out[1] = summed
    out[2] = jnp.broadcast_to(-summed[6:7], (8, n_act))
    out_copy = pltpu.make_async_copy(out, out_hbm, out_sem)
    out_copy.start()
    each(n_dev, lambda k: src_copy(dev, on_dev(k)).wait_send())
    each(n_grp, lambda k: star_copy(grp, on_grp(k)).wait_send())
    each(n_grp, lambda k: part_copy(grp, on_grp(k)).wait_send())
    out_copy.wait()


def hand_out(all_hbm, pos_vel_hbm, acc_jerk_hbm, pot_hbm, sem):
    copies = [
        pltpu.make_async_copy(all_hbm.at[0, 0:6], pos_vel_hbm, sem.at[0]),
        pltpu.make_async_copy(all_hbm.at[1, 0:6], acc_jerk_hbm, sem.at[1]),
        pltpu.make_async_copy(all_hbm.at[2, 0:1], pot_hbm, sem.at[2]),
    ]
    for copy in copies:
        copy.start()
    for copy in copies:
        copy.wait()


def solution(mesh):
    n_grp, n_dev = mesh.shape["grp"], mesh.shape["dev"]

    def shards(positions, velocities, accel_old, jerk_old, masses, levels, live_count, active_slot):
        n_src, n_act = positions.shape[1], active_slot.shape[0]
        n_chunk = n_src // LANES
        hbm = pl.BlockSpec(memory_space=pltpu.HBM)
        args = (
            positions, velocities, accel_old, jerk_old,
            masses[None], levels[None], live_count, active_slot[None],
        )
        f32 = jnp.float32
        dma = pltpu.SemaphoreType.DMA
        params = {"vmem_limit_bytes": 60 * 1024 * 1024}
        everything = pl.pallas_call(
            functools.partial(share, n_grp, n_dev, math.gcd(2, n_dev), math.gcd(4, n_dev)),
            out_shape=jax.ShapeDtypeStruct((3, 8, n_act), f32),
            in_specs=[hbm] * 8,
            out_specs=hbm,
            scratch_shapes=[
                (pltpu.SMEM if a is live_count else pltpu.VMEM)(a.shape, a.dtype) for a in args
            ] + [
                pltpu.VMEM((n_dev, n_chunk, 8, LANES), f32),
                pltpu.VMEM((n_grp, 8, n_act), f32),
                pltpu.VMEM((n_grp, 6, n_act, LANES), f32),
                pltpu.VMEM((7, n_act, LANES), f32),
                pltpu.VMEM((8, n_src), f32),
                pltpu.VMEM((n_grp, 8, n_act), f32),
                pltpu.VMEM((n_grp, 8, n_act), f32),
                pltpu.VMEM((3, 8, n_act), f32),
                dma((8,)),
                dma((n_dev,)), dma((n_dev,)),
                dma((n_grp,)), dma((n_grp,)),
                dma((n_grp,)), dma((n_grp,)),
                dma,
            ],
            compiler_params=pltpu.CompilerParams(
                collective_id=0, has_side_effects=True, **params
            ),
        )(*args)
        pos_vel, acc_jerk, pot = pl.pallas_call(
            hand_out,
            out_shape=(
                jax.ShapeDtypeStruct((6, n_act), f32),
                jax.ShapeDtypeStruct((6, n_act), f32),
                jax.ShapeDtypeStruct((1, n_act), f32),
            ),
            in_specs=[hbm],
            out_specs=(hbm,) * 3,
            scratch_shapes=[dma((3,))],
            compiler_params=pltpu.CompilerParams(**params),
        )(everything)
        return pos_vel, acc_jerk, pot[0]

    split = P(None, ("grp", "dev"))
    flat = P(("grp", "dev"))
    return jax.shard_map(
        shards,
        mesh=mesh,
        in_specs=(split, split, split, split, flat, flat, flat, flat),
        out_specs=(split, split, flat),
        check_vma=False,
    )
```

time: 22.3 us -> 21.4 us (0.960)
  Pallas kernels: 20.9 us -> 19.9 us
    pallas_call x2, Pallas kernels: 20.9 us -> 19.9 us  [the longest x1 18.6 us: shards(): pl.pallas_call(functools.partial(share, n_grp, n_dev, math.gcd(2, n_dev),...]
where the time goes in v3:
time: 21.4 us; the launch traced here: 21.2 us
  Pallas kernels  19.9 us (93%)
  between operations  1.29 us (6%)
    pallas_call x1, Pallas kernels, shards(): pl.pallas_call(functools.partial(share, n_grp, n_dev, math.gcd(2, n_dev),...  18.6 us
    pallas_call x1, Pallas kernels, shards(): pl.pallas_call(hand_out, out_shape=(jax.ShapeDtypeStruct((6, n_act), f32)...  1.33 us

profile of v3, /device:TPU:0, one launch (start us, length us, event | category | flops | bytes accessed | tf_op | source)
XLA Modules:
  0.0 21.2 jit_solution(992294523495947274)
XLA Ops:
  1.3 18.6 %shard_map.103.all_hbm = f32[3,8,128]{2,1,0:T(8,128)} custom-call(f32[3,256]{1,0:T(4,128)} %pos_hbm.1, f32[3,256]{1,0:T(4,128)} %vel_hbm.1, f32[3,256]{1,0:T(4,128)} %acc_hbm.1, f32[3,256]{1,0:T(4,128)} %jerk_hbm.1, f32[1,256]{1,0:T(1,128)} %bitcast.4, s32[1,256]{1,0:T(1,128)} %bitcast.5, s32[1]{0:T(128)S(6)} %copy.11.live_hbm, s32[1,128]{1,0:T(1,128)} %bitcast.6), custom_call_target="tpu_custom_call" | custom-call | tf_op jit(solution)/shard_map/pallas_call | solution.py:272
  19.9 1.3 %shard_map.104 = (f32[6,128]{1,0:T(8,128)}, f32[6,128]{1,0:T(8,128)}, f32[1,128]{1,0:T(1,128)}) custom-call(f32[3,8,128]{2,1,0:T(8,128)} %shard_map.103.all_hbm), custom_call_target="tpu_custom_call" | custom-call | tf_op jit(solution)/shard_map/pallas_call | solution.py:298

commit v4 on v3

--- a/solution.py
+++ b/solution.py
@@ -160,8 +160,9 @@
     old = pick(lambda chunk: rest[:, chunk * LANES : (chunk + 1) * LANES])
 
     def spread(origin):
+        columns = stars[origin].T
         for c in range(6):
-            act[origin, c] = jnp.broadcast_to(stars[origin, c : c + 1, :], (LANES, n_act)).T
+            act[origin, c] = jnp.broadcast_to(columns[:, c : c + 1], (n_act, LANES))
 
     spread(grp)
 
@@ -194,15 +195,17 @@
 
         lax.fori_loop(1, n_dev // batch, turns, 0)
 
-    def total_of(c):
-        return jnp.sum(total[c].T, axis=0, keepdims=True)
+    def summed_up():
+        lane = lax.broadcasted_iota(jnp.int32, (n_act, LANES), 1)
+        columns = jnp.zeros((n_act, LANES), jnp.float32)
+        for c in range(7):
+            columns = jnp.where(lane == c, jnp.sum(total[c], axis=1, keepdims=True), columns)
+        return columns.T[0:8, :]
 
     def give(k, batch, arriving):
         origin = on_grp(k)
         add_all(origin, batch, arriving)
-        for c in range(7):
-            part[origin, c : c + 1, :] = total_of(c)
-        part[origin, 7:8, :] = jnp.zeros((1, n_act), jnp.float32)
+        part[origin] = summed_up()
         part_copy(grp, origin).start()
 
     if n_grp > 1:
@@ -214,9 +217,7 @@
 
     lax.fori_loop(2, n_grp, give_next, 0)
     add_all(grp, many, n_grp == 1)
-    for c in range(7):
-        part[grp, c : c + 1, :] = total_of(c)
-    part[grp, 7:8, :] = jnp.zeros((1, n_act), jnp.float32)
+    part[grp] = summed_up()
 
     def gather(k, summed):
         origin = on_grp(k)
@@ -270,7 +271,7 @@
         dma = pltpu.SemaphoreType.DMA
         params = {"vmem_limit_bytes": 60 * 1024 * 1024}
         everything = pl.pallas_call(
-            functools.partial(share, n_grp, n_dev, math.gcd(2, n_dev), math.gcd(4, n_dev)),
+            functools.partial(share, n_grp, n_dev, math.gcd(4, n_dev), math.gcd(8, n_dev)),
             out_shape=jax.ShapeDtypeStruct((3, 8, n_act), f32),
             in_specs=[hbm] * 8,
             out_specs=hbm,

time: 21.4 us -> 22 us (1.028)
  Pallas kernels: 19.9 us -> 20.5 us
    pallas_call x1, Pallas kernels: 18.6 us -> 19.2 us  [shards(): pl.pallas_call(functools.partial(share, n_grp, n_dev, math.gcd(4, n_dev),...]
where the time goes in v4:
time: 22 us; the launch traced here: 21.8 us
  Pallas kernels  20.5 us (93%)
  between operations  1.29 us (6%)
    pallas_call x1, Pallas kernels, shards(): pl.pallas_call(functools.partial(share, n_grp, n_dev, math.gcd(4, n_dev),...  19.2 us
    pallas_call x1, Pallas kernels, shards(): pl.pallas_call(hand_out, out_shape=(jax.ShapeDtypeStruct((6, n_act), f32)...  1.33 us

profile of v4, /device:TPU:0, one launch (start us, length us, event | category | flops | bytes accessed | tf_op | source)
XLA Modules:
  0.0 21.8 jit_solution(17967430840843263154)
XLA Ops:
  1.3 19.2 %shard_map.103.all_hbm = f32[3,8,128]{2,1,0:T(8,128)} custom-call(f32[3,256]{1,0:T(4,128)} %pos_hbm.1, f32[3,256]{1,0:T(4,128)} %vel_hbm.1, f32[3,256]{1,0:T(4,128)} %acc_hbm.1, f32[3,256]{1,0:T(4,128)} %jerk_hbm.1, f32[1,256]{1,0:T(1,128)} %bitcast.4, s32[1,256]{1,0:T(1,128)} %bitcast.5, s32[1]{0:T(128)S(6)} %copy.11.live_hbm, s32[1,128]{1,0:T(1,128)} %bitcast.6), custom_call_target="tpu_custom_call" | custom-call | tf_op jit(solution)/shard_map/pallas_call | solution.py:273
  20.5 1.3 %shard_map.104 = (f32[6,128]{1,0:T(8,128)}, f32[6,128]{1,0:T(8,128)}, f32[1,128]{1,0:T(1,128)}) custom-call(f32[3,8,128]{2,1,0:T(8,128)} %shard_map.103.all_hbm), custom_call_target="tpu_custom_call" | custom-call | tf_op jit(solution)/shard_map/pallas_call | solution.py:299

commit v5 on v4

--- a/solution.py
+++ b/solution.py
@@ -14,17 +14,22 @@
 SOFTEN_SQ = 0.0001
 
 
-def add_pairs(state, sums, source):
+def meet_pairs(state, source):
     x, y, z, vx, vy, vz = state
-    ax, ay, az, jx, jy, jz, pot = sums
-    sx, sy, sz, svx, svy, svz, mass = source
+    sx, sy, sz, svx, svy, svz = source
     dx, dy, dz = sx - x, sy - y, sz - z
     ex, ey, ez = svx - vx, svy - vy, svz - vz
     inv = lax.rsqrt(dx * dx + dy * dy + dz * dz + SOFTEN_SQ)
+    return dx, dy, dz, ex, ey, ez, dx * ex + dy * ey + dz * ez, inv
+
+
+def add_pairs(sums, pairs, mass):
+    ax, ay, az, jx, jy, jz, pot = sums
+    dx, dy, dz, ex, ey, ez, along, inv = pairs
     inv_sq = inv * inv
     w = mass * inv
     u = w * inv_sq
-    radial = (3.0 * inv_sq) * (dx * ex + dy * ey + dz * ez)
+    radial = (3.0 * inv_sq) * along
     px, py, pz = u * dx, u * dy, u * dz
     return (
         ax + px, ay + py, az + pz,
@@ -33,16 +38,27 @@
     )
 
 
-def sweep(act, total, rows, fresh, chunks):
+def sweep(act, total, rows, n_block, n_chunk, row_of):
     def group(g, carry):
         at = pl.ds(pl.multiple_of(g * rows, rows), rows)
         state = [act[c, at, :] for c in range(6)]
-        if fresh:
-            sums = (jnp.zeros((rows, LANES), jnp.float32),) * 7
-        else:
-            sums = tuple(total[c, at, :] for c in range(7))
-        for chunk in chunks:
-            sums = add_pairs(state, sums, [chunk(c) for c in range(7)])
+
+        def met(block, chunk):
+            return meet_pairs(state, [row_of(block, chunk, c) for c in range(6)])
+
+        def step(block, held):
+            sums, pairs = held
+            for chunk in range(n_chunk):
+                if chunk + 1 < n_chunk:
+                    later = met(block, chunk + 1)
+                else:
+                    later = met(block + 1, 0)
+                sums = add_pairs(sums, pairs, row_of(block, chunk, 6))
+                pairs = later
+            return sums, pairs
+
+        nothing = (jnp.zeros((rows, LANES), jnp.float32),) * 7
+        sums, _ = lax.fori_loop(0, n_block, step, (nothing, met(0, 0)))
         for c in range(7):
             total[c, at, :] = sums[c]
         return carry
@@ -51,7 +67,7 @@
 
 
 def share(
-    n_grp, n_dev, few, many,
+    n_grp, n_dev,
     pos_hbm, vel_hbm, acc_hbm, jerk_hbm, mass_hbm, level_hbm, live_hbm, slot_hbm,
     out_hbm,
     pos_ref, vel_ref, acc_ref, jerk_ref, mass_ref, level_ref, live_ref, slot_ref,
@@ -173,27 +189,11 @@
 
     each(n_grp, meet)
 
-    def add(origin, batch, turn, fresh, arriving):
-        chunks = []
-        for b in range(batch):
-            k = turn * batch + b
-            index = on_dev(k)
-            chunks += [
-                lambda c, index=index, chunk=chunk: src[index, chunk, c : c + 1, :]
-                for chunk in range(n_chunk)
-            ]
-            if arriving and not (fresh and b == 0):
-                src_copy(index, index).wait_recv()
-        sweep(act.at[origin], total, math.gcd(16, n_act), fresh, chunks)
-
-    def add_all(origin, batch, arriving):
-        add(origin, batch, 0, True, arriving)
-
-        def turns(turn, carry):
-            add(origin, batch, turn, False, arriving)
-            return carry
-
-        lax.fori_loop(1, n_dev // batch, turns, 0)
+    def add_all(origin):
+        sweep(
+            act.at[origin], total, math.gcd(16, n_act), n_dev, n_chunk,
+            lambda block, chunk, c: src[on_dev(block), chunk, c : c + 1, :],
+        )
 
     def summed_up():
         lane = lax.broadcasted_iota(jnp.int32, (n_act, LANES), 1)
@@ -202,21 +202,16 @@
             columns = jnp.where(lane == c, jnp.sum(total[c], axis=1, keepdims=True), columns)
         return columns.T[0:8, :]
 
-    def give(k, batch, arriving):
+    each(n_dev, lambda k: src_copy(on_dev(k), on_dev(k)).wait_recv())
+
+    def give(k):
         origin = on_grp(k)
-        add_all(origin, batch, arriving)
+        add_all(origin)
         part[origin] = summed_up()
         part_copy(grp, origin).start()
 
-    if n_grp > 1:
-        give(1, few, True)
-
-    def give_next(k, carry):
-        give(k, many, False)
-        return carry
-
-    lax.fori_loop(2, n_grp, give_next, 0)
-    add_all(grp, many, n_grp == 1)
+    each(n_grp, give)
+    add_all(grp)
     part[grp] = summed_up()
 
     def gather(k, summed):
@@ -271,7 +266,7 @@
         dma = pltpu.SemaphoreType.DMA
         params = {"vmem_limit_bytes": 60 * 1024 * 1024}
         everything = pl.pallas_call(
-            functools.partial(share, n_grp, n_dev, math.gcd(4, n_dev), math.gcd(8, n_dev)),
+            functools.partial(share, n_grp, n_dev),
             out_shape=jax.ShapeDtypeStruct((3, 8, n_act), f32),
             in_specs=[hbm] * 8,
             out_specs=hbm,

time: 22 us -> 23.3 us (1.059)
  Pallas kernels: 20.5 us -> 21.8 us
    pallas_call x1, Pallas kernels: 19.2 us -> 20.5 us  [shards(): pl.pallas_call(functools.partial(share, n_grp, n_dev), out_shape=jax.Shap...]
where the time goes in v5:
time: 23.3 us; the launch traced here: 23.1 us
  Pallas kernels  21.8 us (94%)
  between operations  1.29 us (6%)
    pallas_call x1, Pallas kernels, shards(): pl.pallas_call(functools.partial(share, n_grp, n_dev), out_shape=jax.Shap...  20.5 us
    pallas_call x1, Pallas kernels, shards(): pl.pallas_call(hand_out, out_shape=(jax.ShapeDtypeStruct((6, n_act), f32)...  1.33 us

profile of v5, /device:TPU:0, one launch (start us, length us, event | category | flops | bytes accessed | tf_op | source)
XLA Modules:
  0.0 23.1 jit_solution(17683151315181419919)
XLA Ops:
  1.3 20.5 %shard_map.103.all_hbm = f32[3,8,128]{2,1,0:T(8,128)} custom-call(f32[3,256]{1,0:T(4,128)} %pos_hbm.1, f32[3,256]{1,0:T(4,128)} %vel_hbm.1, f32[3,256]{1,0:T(4,128)} %acc_hbm.1, f32[3,256]{1,0:T(4,128)} %jerk_hbm.1, f32[1,256]{1,0:T(1,128)} %bitcast.4, s32[1,256]{1,0:T(1,128)} %bitcast.5, s32[1]{0:T(128)S(6)} %copy.11.live_hbm, s32[1,128]{1,0:T(1,128)} %bitcast.6), custom_call_target="tpu_custom_call" | custom-call | tf_op jit(solution)/shard_map/pallas_call | solution.py:268
  21.7 1.3 %shard_map.104 = (f32[6,128]{1,0:T(8,128)}, f32[6,128]{1,0:T(8,128)}, f32[1,128]{1,0:T(1,128)}) custom-call(f32[3,8,128]{2,1,0:T(8,128)} %shard_map.103.all_hbm), custom_call_target="tpu_custom_call" | custom-call | tf_op jit(solution)/shard_map/pallas_call | solution.py:294
